TPU v7x, 32 devices: a whole 2x2x4 slice. The times are simulated.
32 devices in a mesh: dp: 8 (over z, core), proto: 4 (over y, x).
Axes of the slice: x: 2, y: 2, z: 4, core: 2. Of those that a mesh axis runs over, the one named last changes fastest.
Arguments:
- student_rows: bfloat16 [32, 256, 256], P('dp'), may hold values from -8 to 8
- teacher_rows: bfloat16 [32, 256, 256], P('dp'), may hold values from -8 to 8
- prototypes: bfloat16 [256, 131072], P(None, 'proto'), may hold values from -8 to 8
- center: float32 [131072], P('proto'), may hold values from -1.2 to 1.2
- mask_index: int32 [32, 128], P('dp'), may hold values from 0 to 255, as said below
- mask_count: int32 [32], P('dp'), may hold values from 0 to 128, as said below
- loss_scale: float32 [], replicated, may hold values from 1024 to 4096
Outputs:
- loss: float32 [], replicated
- student_grad: float32 [32, 256, 256], P('dp')
- proto_grad: float32 [131072, 256], P(('proto', 'dp'))
- patch_center: float32 [131072], P('proto')
Inputs may be any that keep to these rules, and one draw needn't show every extreme that they name: `mask_index`: for each image the first mask_count entries are distinct patch numbers; the later entries are patch numbers that are ignored. `mask_count`: the counts of all 32 images sum to 2048; some images have no masked patch.
All inputs are finite; a program needn't handle non-finite values.
Results may differ from a plain program's by a relative error of at most 0.022.
Values may be sent and summed in bfloat16 or wider, within the bound.
A program may use at most 256 MiB of HBM per device.

v0:
```python
import jax
import jax.numpy as jnp
from jax import lax
from jax.sharding import PartitionSpec as P

teacher_temp = 0.04
student_temp = 0.1
norm_epsilon = 1e-06


def joined(value, axis, join):
    pieces = jax.tree.map(lambda part: lax.all_gather(part, axis), value)
    head = jax.tree.map(lambda part: part[0], pieces)
    tail = jax.tree.map(lambda part: part[1:], pieces)
    so_far, _ = lax.scan(lambda so_far, slab: (join(so_far, slab), None), head, tail)
    return so_far


def unit_rows(raw):
    values = raw.astype(jnp.float32)
    length = jnp.sqrt(jnp.sum(values * values, axis=1, keepdims=True) + norm_epsilon)
    return (values / length, length)


def merge_stats(first, second):
    t_top = jnp.maximum(first[0], second[0])
    t_left = jnp.exp(first[0] - t_top)
    t_right = jnp.exp(second[0] - t_top)
    s_top = jnp.maximum(first[3], second[3])
    s_left = jnp.exp(first[3] - s_top)
    s_right = jnp.exp(second[3] - s_top)
    return (
        t_top,
        first[1] * t_left + second[1] * t_right,
        first[2] * t_left + second[2] * t_right,
        s_top,
        first[4] * s_left + second[4] * s_right,
    )


def norm_backward(d_unit, s_unit, s_len):
    return (d_unit - s_unit * jnp.sum(s_unit * d_unit, axis=1, keepdims=True)) / s_len


def shards(student_rows, teacher_rows, prototypes, center, mask_index, mask_count, loss_scale):
    img_local, patches, width = student_rows.shape
    max_masked = mask_index.shape[1]
    data_size = lax.axis_size("dp")
    images = img_local * data_size
    padded_rows = img_local * max_masked
    total = images * max_masked // 2
    slots = jnp.arange(max_masked, dtype=jnp.int32)
    valid = slots[None, :] < mask_count[:, None]
    flat_valid = valid.reshape(-1)
    image_ids = jnp.arange(img_local, dtype=jnp.int32)[:, None]
    picked_s = student_rows[image_ids, mask_index].reshape(padded_rows, width)
    picked_t = teacher_rows[image_ids, mask_index].reshape(padded_rows, width)
    s_rows, t_rows = (picked_s, picked_t)
    count_f = jnp.maximum(mask_count, 1).astype(jnp.float32)
    weight = jnp.where(valid, 1.0 / (images * count_f[:, None]), 0.0).reshape(-1)
    live = flat_valid.astype(jnp.float32)
    s_unit, s_len = unit_rows(s_rows)
    t_unit, t_len = unit_rows(t_rows)
    s_half = s_unit.astype(jnp.bfloat16)
    t_half = t_unit.astype(jnp.bfloat16)
    s_logit = jnp.dot(s_half, prototypes, preferred_element_type=jnp.float32)
    t_logit = jnp.dot(t_half, prototypes, preferred_element_type=jnp.float32)
    col_sum = jnp.sum(t_logit * live[:, None], axis=0)
    t_arg = (t_logit - center[None, :]) / teacher_temp
    t_top = jnp.max(t_arg, axis=1)
    t_exp = jnp.exp(t_arg - t_top[:, None])
    s_arg = s_logit / student_temp
    s_top = jnp.max(s_arg, axis=1)
    s_exp = jnp.exp(s_arg - s_top[:, None])
    local_stats = (
        t_top,
        jnp.sum(t_exp, axis=1),
        jnp.sum(t_exp * s_arg, axis=1),
        s_top,
        jnp.sum(s_exp, axis=1),
    )
    t_all, t_total, cross, s_all, s_total = joined(local_stats, "proto", merge_stats)
    t_prob = t_exp * (jnp.exp(t_top - t_all) / t_total)[:, None]
    s_prob = s_exp * (jnp.exp(s_top - s_all) / s_total)[:, None]
    s_lse = s_all + jnp.log(s_total)
    ce = s_lse - cross / t_total
    loss_part = jnp.sum(weight * ce)
    col_total, loss = (
        lax.psum(col_sum.astype(jnp.bfloat16), "dp").astype(jnp.float32),
        lax.psum(loss_part.astype(jnp.bfloat16), "dp").astype(jnp.float32),
    )
    patch_center = col_total / total
    dlogit = (loss_scale * weight[:, None] * (s_prob - t_prob) / student_temp).astype(jnp.bfloat16)
    proto_grad = lax.psum_scatter(
        lax.dot_general(
            dlogit, s_half, (((0,), (0,)), ((), ())), preferred_element_type=jnp.float32
        ),
        "dp",
        scatter_dimension=0,
        tiled=True,
    )
    d_part = lax.dot_general(
        dlogit, prototypes, (((1,), (1,)), ((), ())), preferred_element_type=jnp.float32
    )
    d_unit = lax.psum(d_part, "proto")
    row_grads = norm_backward(d_unit, s_unit, s_len)
    rows_back = row_grads * live[:, None]
    student_grad = (
        jnp.zeros((img_local, patches, width), jnp.float32)
        .at[image_ids, mask_index]
        .add(rows_back.reshape(img_local, max_masked, width))
    )
    return (loss, student_grad, proto_grad, patch_center)


def solution(mesh):
    in_specs = (
        P("dp", None, None),
        P("dp", None, None),
        P(None, "proto"),
        P("proto"),
        P("dp", None),
        P("dp"),
        P(),
    )
    out_specs = (P(), P("dp", None, None), P(("proto", "dp"), None), P("proto"))
    return jax.shard_map(shards, mesh=mesh, in_specs=in_specs, out_specs=out_specs, check_vma=False)
```

profile of v0, /device:TPU:0, one launch (start us, length us, event | category | flops | bytes accessed | tf_op | source)
XLA Modules:
  0.0 626.6 jit_solution(9647993426960283608)
XLA Ops:
  7.2 1.3 select_bitcast_fusion
  8.5 3.2 gather_fusion.1
  11.9 7.0 %gather_fusion = bf16[512,256]{1,0:T(8,128)(2,1)S(1)} fusion(bf16[4,256,256]{2,1,0:T(8,128)(2,1)} %param.10, s32[512]{0:T(512)S(1)} %get-tuple-element.106), kind=kCustom, calls=%fused_computation | custom fusion | bytes 528384 | tf_op jit(solution)/shard_map/gather | solution.py:57
  19.0 0.7 convert_bitcast_fusion
  19.8 29.1 %multiply_reduce_fusion.2 = (f32[512]{0:T(512)S(1)}, f32[512,32768]{1,0:T(8,128)}) fusion(bf16[256,32768]{1,0:T(8,128)(2,1)} %param.11, f32[512]{0:T(512)S(1)} %add_sqrt_fusion, bf16[512,256]{1,0:T(8,128)(2,1)S(1)} %gather_fusion.1), kind=kOutput, calls=%fused_computation.21 | convolution fusion | flops 8623882240 | bytes 84152320 | tf_op jit(solution)/shard_map/dot_general | solution.py:66
  48.8 30.0 %fusion = (f32[512]{0:T(512)S(1)}, f32[512,32768]{1,0:T(8,128)}) fusion(f32[32768]{0:T(1024)S(1)} %copy-done.4, bf16[256,32768]{1,0:T(8,128)(2,1)} %param.11, bf16[512,256]{1,0:T(8,128)(2,1)S(1)} %gather_fusion, f32[512]{0:T(512)S(1)} %add_sqrt_fusion.1), kind=kOutput, calls=%fused_computation.19 | convolution fusion | flops 8640659456 | bytes 84283392 | tf_op jit(solution)/shard_map/dot_general | solution.py:67
  78.9 50.7 %multiply_reduce_fusion.1 = (f32[512]{0:T(512)S(1)}, f32[512]{0:T(512)S(1)}, bf16[32768]{0:T(1024)(128)(2,1)}, f32[512]{0:T(512)S(1)}) fusion(f32[512,32768]{1,0:T(8,128)} %get-tuple-element.111, f32[512,32768]{1,0:T(8,128)} %get-tuple-element.109, f32[512]{0:T(512)S(1)} %get-tuple-element.108, f32[32768]{0:T(1024)S(1)} %copy-done.4, ...), kind=kLoop, calls=%fused_computation.16 | loop fusion | flops 184515072 | bytes 134426624 | tf_op jit(solution)/shard_map/reduce_sum | solution.py:78
  129.7 9.5 %all-gather.6 = f32[4,1,512]{2,1,0:T(1,128)S(1)} all-gather(f32[1,1,512]{2,1,0:T(1,128)S(1)} %bitcast.86), channel_id=3, replica_groups=mesh['dp'=8,'proto'=4] {'proto'}, dimensions={0}, use_global_device_ids=true | all-gather | bytes 10240 | tf_op jit(solution)/shard_map/all_gather | solution.py:12
  139.2 8.0 %all-gather.7 = f32[4,1,512]{2,1,0:T(1,128)S(1)} all-gather(f32[1,1,512]{2,1,0:T(1,128)S(1)} %bitcast.85), channel_id=4, replica_groups=mesh['dp'=8,'proto'=4] {'proto'}, dimensions={0}, use_global_device_ids=true | all-gather | bytes 10240 | tf_op jit(solution)/shard_map/all_gather | solution.py:12
  147.2 7.1 %all-gather.9 = f32[4,1,512]{2,1,0:T(1,128)S(1)} all-gather(f32[1,1,512]{2,1,0:T(1,128)S(1)} %bitcast.84), channel_id=6, replica_groups=mesh['dp'=8,'proto'=4] {'proto'}, dimensions={0}, use_global_device_ids=true | all-gather | bytes 10240 | tf_op jit(solution)/shard_map/all_gather | solution.py:12
  154.3 8.0 %all-gather.8 = f32[4,1,512]{2,1,0:T(1,128)S(1)} all-gather(f32[1,1,512]{2,1,0:T(1,128)S(1)} %bitcast.77), channel_id=5, replica_groups=mesh['dp'=8,'proto'=4] {'proto'}, dimensions={0}, use_global_device_ids=true | all-gather | bytes 10240 | tf_op jit(solution)/shard_map/all_gather | solution.py:12
  162.4 7.3 %all-gather.5 = f32[4,1,512]{2,1,0:T(1,128)S(1)} all-gather(f32[1,1,512]{2,1,0:T(1,128)S(1)} %bitcast.78), channel_id=2, replica_groups=mesh['dp'=8,'proto'=4] {'proto'}, dimensions={0}, use_global_device_ids=true | all-gather | bytes 10240 | tf_op jit(solution)/shard_map/all_gather | solution.py:12
  169.8 0.5 while.18
  170.9 0.7 exponential_divide_fusion.1
  171.5 53.5 %multiply_convert_fusion = bf16[512,32768]{1,0:T(8,128)(2,1)} fusion(f32[512,32768]{1,0:T(8,128)} %get-tuple-element.111, f32[512,32768]{1,0:T(8,128)} %get-tuple-element.109, f32[512]{0:T(512)S(1)} %get-tuple-element.104, f32[512]{0:T(512)S(1)} %get-tuple-element.102, f32[512]{0:T(512)S(1)} %get-tuple-element.107, f32[512]{0:T(512)S(1)} %get-tuple-element.110, ...), kind=kLoop, calls=%fused_computation.14 | loop fusion | flops 184549376 | bytes 167913472 | tf_op jit(solution)/shard_map/convert_element_type | solution.py:93
  225.0 19.5 %fusion.19 = f32[512,256]{1,0:T(8,128)} fusion(bf16[512,32768]{1,0:T(8,128)(2,1)} %multiply_convert_fusion, bf16[256,32768]{1,0:T(8,128)(2,1)} %param.11), kind=kOutput, calls=%fused_computation.65 | convolution fusion | flops 8589934592 | bytes 50855936 | tf_op jit(solution)/shard_map/dot_general | solution.py:102
  244.6 26.5 %fusion.9 = f32[32768,256]{1,0:T(8,128)} fusion(bf16[512,32768]{1,0:T(8,128)(2,1)} %multiply_convert_fusion, bf16[512,256]{1,0:T(8,128)(2,1)S(1)} %gather_fusion.1, f32[512]{0:T(512)S(1)} %add_sqrt_fusion), kind=kOutput, calls=%fused_computation.35 | convolution fusion | flops 8590327808 | bytes 67373056 | tf_op jit(solution)/shard_map/dot_general | solution.py:95
  271.1 14.3 %psum.21 = bf16[]{:T(256)} all-reduce(bf16[]{:T(256)} %get-tuple-element.103), channel_id=1, replica_groups=mesh['dp'=8,'proto'=4] {'dp'}, use_global_device_ids=true, to_apply=%region_10.11 | all-reduce | flops 1 | bytes 4 | tf_op jit(solution)/shard_map/psum | solution.py:90
  286.1 1.5 convert_multiply_fusion.2
  287.6 2.7 all-reduce.3.cloned.1.call-done
  290.3 1.3 multiply_reduce_fusion.3
  291.6 1.3 divide_multiply_fusion
  293.0 26.2 %scatter_fusion = f32[4,256,256]{2,1,0:T(8,128)S(1)} fusion(f32[4,256,256]{2,1,0:T(8,128)S(1)} %broadcast_in_dim.22, s32[512]{0:T(512)S(1)} %copy-done.2, f32[512,256]{1,0:T(8,128)S(1)} %divide_multiply_fusion), kind=kCustom, calls=%fused_computation.2 | custom fusion | flops 131072 | bytes 1576960 | tf_op jit(solution)/shard_map/scatter-add | solution.py:111
  319.2 299.7 %reduce-scatter.2.cloned.1.call-done = f32[4096,256]{1,0:T(8,128)} async-done(((f32[32768,256]{1,0:T(8,128)}), f32[4096,256]{1,0:T(8,128)}) %reduce-scatter.2.cloned.1.call-update) | async-done | bytes 4194320 | tf_op jit(solution)/shard_map/reduce_scatter | solution.py:94
  (64 shorter events, 0.9 us)
Async XLA Ops:
  7.2 1.4 copy-start
  7.2 41.7 %copy-start.4 = (f32[32768]{0:T(1024)S(1)}, f32[32768]{0:T(1024)}, u32[]{:S(2)}) copy-start(f32[32768]{0:T(1024)} %param.12) | copy-start | bytes 393220
  7.2 278.9 %all-reduce.5.cloned.1.call-start = ((), (), s32[]{:S(2)}) async-start(), calls=%async_computation.3 | async-start | bytes 131072 | tf_op jit(solution)/shard_map/psum | solution.py:89
  78.9 90.8 %copy-start.5 = (s32[4]{0:T(128)S(1)}, s32[4]{0:T(128)}, u32[]{:S(2)}) copy-start(s32[4]{0:T(128)} %param.14) | copy-start | bytes 52
  129.6 160.7 %all-reduce.3.cloned.1.call-start = ((), (), s32[]{:S(2)}) async-start(), calls=%async_computation.1 | async-start | bytes 1048576 | tf_op jit(solution)/shard_map/psum | solution.py:105
  225.0 394.0 %copy-start.1 = (bf16[4,256,256]{2,1,0:T(8,128)(2,1)S(1)}, bf16[4,256,256]{2,1,0:T(8,128)(2,1)}, u32[]{:S(2)}) copy-start(bf16[4,256,256]{2,1,0:T(8,128)(2,1)} %param.9) | copy-start | bytes 1572868
  244.5 48.5 %copy-start.2 = (s32[512]{0:T(512)S(1)}, s32[512]{0:T(512)}, u32[]{:S(2)}) copy-start(s32[512]{0:T(512)} %get-tuple-element.105) | copy-start | bytes 6148
  244.5 374.4 %reduce-scatter.2.cloned.1.call-start = ((), (), s32[]{:S(2)}) async-start(), calls=%async_computation.2 | async-start | bytes 37748736 | tf_op jit(solution)/shard_map/reduce_scatter | solution.py:94
  319.2 299.8 %copy-start.3 = (f32[4,256,256]{2,1,0:T(8,128)}, f32[4,256,256]{2,1,0:T(8,128)S(1)}, u32[]{:S(2)}) copy-start(f32[4,256,256]{2,1,0:T(8,128)S(1)} %scatter_fusion) | copy-start | bytes 3145732
Sparse Core Ops, SparseCore 0:
  129.7 56.3 all-reduce.4
  244.7 45.6 all-reduce.2
  293.4 325.5 reduce-scatter.1
where the time goes:
time: 627 us
  waiting for transfers between devices  302 us (48%)
  other arithmetic  138 us (22%)
  matrix products  105 us (17%)
  blocking collectives  54.3 us (9%)
  between operations  16.4 us (3%)
  local copies, waits for them, and re-layouts  10.5 us (2%)
    reduce_scatter x1, waiting for transfers between devices, shards(): lax.psum_scatter(lax.dot_general(dlogit, s_half, (((0,), (0,)), ((), ()))...  300 us
    convert_element_type x1, other arithmetic, shards(): (loss_scale * weight[:, None] * (s_prob - t_prob) / student_temp).astype(...  53.5 us
    reduce_sum x1, other arithmetic, shards(): jnp.sum(t_exp * s_arg, axis=1)  50.7 us
    all_gather x5, blocking collectives, joined(): pieces = jax.tree.map(lambda part: lax.all_gather(part, axis), value)  40 us
    dot_general x1, matrix products, shards(): t_logit = jnp.dot(t_half, prototypes, preferred_element_type=jnp.float32)  30 us
    dot_general x1, matrix products, shards(): s_logit = jnp.dot(s_half, prototypes, preferred_element_type=jnp.float32)  29.1 us
    dot_general x1, matrix products, shards(): lax.dot_general(dlogit, s_half, (((0,), (0,)), ((), ())), preferred_eleme...  26.5 us
    scatter-add x1, other arithmetic, shards(): student_grad = jnp.zeros((img_local, patches, width), jnp.float32).at[ima...  26.2 us
  transfers between devices with their start and end apart: 3, of which 2 were waited for; matrix products, arithmetic and copies ran while one was open for 21% of the time, Pallas kernels for 0%

commit v1 on v0

v1 whole, which is shorter than its diff:
```python
import functools
import math

import jax
import jax.numpy as jnp
from jax import lax
from jax.experimental import pallas as pl
from jax.experimental.pallas import tpu as pltpu
from jax.sharding import PartitionSpec as P

teacher_temp = 0.04
student_temp = 0.1
norm_epsilon = 1e-06
log2_e = math.log2(math.e)
ln_2 = math.log(2.0)
tail_rows = 16
vmem_bytes = 56 * 1024 * 1024
f32 = jnp.float32
bf16 = jnp.bfloat16


def unit_rows(raw):
    values = raw.astype(f32)
    length = jnp.sqrt(jnp.sum(values * values, axis=1, keepdims=True) + norm_epsilon)
    return (values / length, length)


def norm_backward(d_unit, s_unit, s_len):
    return (d_unit - s_unit * jnp.sum(s_unit * d_unit, axis=1, keepdims=True)) / s_len


def compact_kernel(max_masked, starts_ref, rows_ref, s_ref, t_ref, held):
    devices, piece, both = rows_ref.shape
    piece -= tail_rows
    total, width = s_ref.shape
    chunk = min(piece, max_masked)

    @pl.loop(0, devices * piece // chunk)
    def _(step):
        flat = step * chunk
        image = flat // max_masked
        at = starts_ref[image] + flat % max_masked
        row = pl.multiple_of(flat % piece, chunk)
        base = pl.multiple_of(at // 8 * 8, 8)
        ahead = at - base
        value = rows_ref[flat // piece, pl.ds(row, chunk), :].astype(f32)
        value = jnp.concatenate([value, jnp.zeros((8, both), f32)], axis=0)
        value = pltpu.roll(value, ahead, 0)
        older = lax.broadcasted_iota(jnp.int32, (8, both), 0) < ahead
        held[pl.ds(base, 8), :] = jnp.where(older, held[pl.ds(base, 8), :], value[:8])
        held[pl.ds(pl.multiple_of(base + 8, 8), chunk), :] = value[8:]

    s_ref[...] = held[:total, :width].astype(bf16)
    t_ref[...] = held[:total, width:].astype(bf16)


def compact(rows, starts, max_masked, total, width):
    return pl.pallas_call(
        functools.partial(compact_kernel, max_masked),
        out_shape=[jax.ShapeDtypeStruct((total, width), bf16)] * 2,
        in_specs=[
            pl.BlockSpec(memory_space=pltpu.SMEM),
            pl.BlockSpec(memory_space=pltpu.VMEM),
        ],
        out_specs=[pl.BlockSpec(memory_space=pltpu.VMEM)] * 2,
        scratch_shapes=[pltpu.VMEM((total + max_masked + 8, 2 * width), f32)],
        compiler_params=pltpu.CompilerParams(vmem_limit_bytes=vmem_bytes),
        name="compact_rows",
    )(starts, rows)


def nt_dot(left, right):
    return lax.dot_general(left, right, (((1,), (1,)), ((), ())), preferred_element_type=f32)


def forward_kernel(s_ref, t_ref, pt_ref, p_ref, c_ref, us_ref, ut_ref, as_ref, at_ref, stat_ref, s_arg, t_arg):
    cols, rows = s_arg.shape
    width = p_ref.shape[0]
    chunk = min(512, cols)
    chunks = [pl.ds(k * chunk, chunk) for k in range(cols // chunk)]
    s_rows = s_ref[...]
    t_rows = t_ref[...]
    lanes = c_ref.shape[1]

    def fold(value):
        return value.reshape(chunk // 8, 8, rows)

    t_top = jnp.full((8, rows), -jnp.inf, f32)
    for part in chunks:
        shift = jnp.concatenate([c_ref[part, :]] * (rows // lanes), axis=1)
        arg = nt_dot(pt_ref[part, :], t_rows) * (log2_e / teacher_temp) - shift
        t_arg[part, :] = arg
        t_top = jnp.maximum(t_top, jnp.max(fold(arg), axis=0))
    t_top = jnp.max(t_top, axis=0, keepdims=True)

    s_top = jnp.full((8, rows), -jnp.inf, f32)
    t_sum = jnp.zeros((8, rows), f32)
    t_acc = jnp.zeros((width, rows), f32)
    for part in chunks:
        arg = nt_dot(pt_ref[part, :], s_rows) * (log2_e / student_temp)
        s_arg[part, :] = arg
        s_top = jnp.maximum(s_top, jnp.max(fold(arg), axis=0))
        grown = jnp.exp2(t_arg[part, :] - t_top)
        t_sum = t_sum + jnp.sum(fold(grown), axis=0)
        half = grown.astype(bf16)
        ut_ref[part, :] = half
        t_acc = t_acc + jnp.dot(p_ref[:, part], half, preferred_element_type=f32)
    s_top = jnp.max(s_top, axis=0, keepdims=True)

    s_sum = jnp.zeros((8, rows), f32)
    s_acc = jnp.zeros((width, rows), f32)
    for part in chunks:
        grown = jnp.exp2(s_arg[part, :] - s_top)
        s_sum = s_sum + jnp.sum(fold(grown), axis=0)
        half = grown.astype(bf16)
        us_ref[part, :] = half
        s_acc = s_acc + jnp.dot(p_ref[:, part], half, preferred_element_type=f32)

    at_ref[...] = t_acc.T
    as_ref[...] = s_acc.T
    cross = jnp.sum(t_acc * s_rows.astype(f32).T, axis=0, keepdims=True)
    stat_ref[...] = jnp.concatenate(
        [
            t_top,
            jnp.sum(t_sum, axis=0, keepdims=True),
            cross,
            s_top,
            jnp.sum(s_sum, axis=0, keepdims=True),
            jnp.zeros((3, rows), f32),
        ],
        axis=0,
    )


def forward(s_half, t_half, protos_t, protos, shift):
    total, width = s_half.shape
    cols = protos.shape[1]
    block = 256
    whole = lambda shape: pl.BlockSpec(shape, lambda i: (0, 0))
    by_row = pl.BlockSpec((block, width), lambda i: (i, 0))
    by_lane = lambda height: pl.BlockSpec((height, block), lambda i: (0, i))
    return pl.pallas_call(
        forward_kernel,
        grid=(total // block,),
        in_specs=[by_row, by_row, whole((cols, width)), whole((width, cols)), whole(shift.shape)],
        out_specs=[by_lane(cols), by_lane(cols), by_row, by_row, by_lane(8)],
        out_shape=[
            jax.ShapeDtypeStruct((cols, total), bf16),
            jax.ShapeDtypeStruct((cols, total), bf16),
            jax.ShapeDtypeStruct((total, width), f32),
            jax.ShapeDtypeStruct((total, width), f32),
            jax.ShapeDtypeStruct((8, total), f32),
        ],
        scratch_shapes=[pltpu.VMEM((cols, block), f32)] * 2,
        compiler_params=pltpu.CompilerParams(vmem_limit_bytes=vmem_bytes),
        cost_estimate=pl.CostEstimate(
            flops=8 * total * width * cols,
            bytes_accessed=4 * total * cols,
            transcendentals=2 * total * cols,
        ),
        name="forward_rows",
    )(s_half, t_half, protos_t, protos, shift)


def proto_grad_kernel(us_ref, ut_ref, s_ref, t_ref, out_ref):
    out_ref[...] = jnp.dot(us_ref[...], s_ref[...], preferred_element_type=f32) - jnp.dot(
        ut_ref[...], t_ref[...], preferred_element_type=f32
    )


def proto_grad_call(us, ut, s_scaled, t_scaled):
    cols, total = us.shape
    width = s_scaled.shape[1]
    block = min(512, cols)
    tall = pl.BlockSpec((block, total), lambda i: (i, 0))
    whole = pl.BlockSpec((total, width), lambda i: (0, 0))
    return pl.pallas_call(
        proto_grad_kernel,
        grid=(cols // block,),
        in_specs=[tall, tall, whole, whole],
        out_specs=pl.BlockSpec((block, width), lambda i: (i, 0)),
        out_shape=jax.ShapeDtypeStruct((cols, width), f32),
        compiler_params=pltpu.CompilerParams(vmem_limit_bytes=vmem_bytes),
        cost_estimate=pl.CostEstimate(
            flops=4 * total * width * cols, bytes_accessed=4 * total * cols, transcendentals=0
        ),
        name="proto_grad_rows",
    )(us, ut, s_scaled, t_scaled)


def shards(student_rows, teacher_rows, prototypes, center, mask_index, mask_count, loss_scale):
    img_local, patches, width = student_rows.shape
    max_masked = mask_index.shape[1]
    data_size = lax.axis_size("dp")
    proto_size = lax.axis_size("proto")
    me_data = lax.axis_index("dp")
    me_proto = lax.axis_index("proto")
    images = img_local * data_size
    padded_rows = img_local * max_masked
    total = images * max_masked // 2
    cols = prototypes.shape[1] // data_size
    piece = padded_rows // proto_size

    patch_ids = jnp.arange(patches, dtype=jnp.int32)
    pick = (mask_index[:, :, None] == patch_ids).astype(bf16)
    both = jnp.concatenate([student_rows, teacher_rows], axis=2)
    picked = jnp.einsum("isp,ipd->isd", pick, both, preferred_element_type=f32)
    picked = picked.reshape(padded_rows, 2 * width)
    s_unit, s_len = unit_rows(picked[:, :width])
    t_unit, _ = unit_rows(picked[:, width:])
    halves = jnp.concatenate([s_unit.astype(bf16), t_unit.astype(bf16)], axis=1)

    mine = lax.dynamic_slice_in_dim(halves, me_proto * piece, piece, axis=0)
    counts_row = jnp.pad(mask_count.astype(bf16)[None, :], ((0, tail_rows - 1), (0, 2 * width - img_local)))
    sent = jnp.concatenate([mine, counts_row], axis=0)
    everyone = lax.all_gather(sent, ("dp", "proto"))
    counts = everyone[::proto_size, piece, :img_local].astype(jnp.int32).reshape(images)
    ends = jnp.cumsum(counts)
    starts = ends - counts
    s_half, t_half = compact(everyone, starts, max_masked, total, width)

    rank = jnp.arange(total, dtype=jnp.int32)[None, :]
    inside = (starts[:, None] <= rank) & (rank < ends[:, None])
    image_weight = 1.0 / (images * jnp.maximum(counts, 1).astype(f32))
    weight = jnp.sum(jnp.where(inside, image_weight[:, None], 0.0), axis=0)

    protos = lax.dynamic_slice_in_dim(prototypes, me_data * cols, cols, axis=1)
    my_center = lax.dynamic_slice_in_dim(center, me_data * cols, cols, axis=0)
    shift = jnp.broadcast_to((my_center * (log2_e / teacher_temp))[:, None], (cols, 128))
    us, ut, s_acc, t_acc, stats = forward(s_half, t_half, protos.T, protos, shift)

    all_stats = lax.all_gather(stats[:5], ("dp", "proto"))
    t_top, t_sum, cross, s_top, s_sum = (all_stats[:, k] for k in range(5))
    t_all = jnp.max(t_top, axis=0)
    s_all = jnp.max(s_top, axis=0)
    t_scale = jnp.exp2(t_top - t_all)
    t_total = jnp.sum(t_sum * t_scale, axis=0)
    s_total = jnp.sum(s_sum * jnp.exp2(s_top - s_all), axis=0)
    cross_mean = jnp.sum(cross * t_scale, axis=0) / t_total
    ce = ln_2 * (s_all + jnp.log2(s_total)) - cross_mean / student_temp
    loss = jnp.sum(weight * ce)

    coef = loss_scale * weight / student_temp
    s_factor = (coef * jnp.exp2(stats[3] - s_all) / s_total)[:, None]
    t_factor = (coef * jnp.exp2(stats[0] - t_all) / t_total)[:, None]
    d_part = (s_factor * s_acc - t_factor * t_acc).astype(bf16)
    d_all = lax.psum(d_part, ("dp", "proto"))

    s_wide = s_half.astype(f32)
    proto_grad = proto_grad_call(us, ut, (s_wide * s_factor).astype(bf16), (s_wide * t_factor).astype(bf16))

    t_rows_sum = jnp.sum(t_half.astype(f32), axis=0) / total
    high = lax.reduce_precision(t_rows_sum, 8, 7)
    rest = t_rows_sum - high
    middle = lax.reduce_precision(rest, 8, 7)
    parts = jnp.stack([high, middle, rest - middle]).astype(bf16)
    parts = jnp.pad(parts, ((0, 5), (0, 0)))
    patch_center = jnp.sum(jnp.dot(parts, prototypes, preferred_element_type=f32), axis=0)

    d_all = jnp.pad(d_all, ((0, max_masked), (0, 0)))
    my_starts = lax.dynamic_slice_in_dim(starts, me_data * img_local, img_local)
    d_unit = jnp.concatenate(
        [lax.dynamic_slice_in_dim(d_all, my_starts[i], max_masked, axis=0) for i in range(img_local)]
    ).astype(f32)
    row_grads = norm_backward(d_unit, s_unit, s_len).reshape(img_local, max_masked, width)
    slots = jnp.arange(max_masked, dtype=jnp.int32)
    valid = slots[None, :] < mask_count[:, None]
    place = (pick * valid[:, :, None].astype(bf16)).astype(f32)
    student_grad = jnp.einsum(
        "isp,isd->ipd", place, row_grads, precision=lax.Precision.HIGHEST, preferred_element_type=f32
    )
    return (loss, student_grad, proto_grad, patch_center)


def solution(mesh):
    in_specs = (
        P("dp", None, None),
        P("dp", None, None),
        P(None, "proto"),
        P("proto"),
        P("dp", None),
        P("dp"),
        P(),
    )
    out_specs = (P(), P("dp", None, None), P(("proto", "dp"), None), P("proto"))
    return jax.shard_map(shards, mesh=mesh, in_specs=in_specs, out_specs=out_specs, check_vma=False)
```

time: 627 us -> 334 us (0.53)
  other arithmetic: 138 us -> 15.2 us
  waiting for transfers between devices: 302 us -> 207 us
  matrix products: 105 us -> 11.9 us
  Pallas kernels: 0 us -> 63.5 us
  blocking collectives: 54.3 us -> 0 us
    reduce_scatter x1 -> x0, waiting for transfers between devices: 300 us -> none  [shards(): lax.psum_scatter(lax.dot_general(dlogit, s_half, (((0,), (0,)), ((), ()))...]
    psum x2 -> x1, waiting for transfers between devices: 2.7 us -> 111 us  [shards(): d_all = lax.psum(d_part, ('dp', 'proto'))]
    all_gather x0 -> x2, waiting for transfers between devices: none -> 95.7 us  [the longest x1 59.7 us: shards(): everyone = lax.all_gather(sent, ('dp', 'proto'))]
    dot_general x4 -> x3, matrix products: 105 us -> 11.9 us  [the longest x1 8.73 us: shards(): jnp.dot(parts, prototypes, preferred_element_type=f32)]
    pallas_call x0 -> x3, Pallas kernels: none -> 63.5 us  [the longest x1 38.5 us: forward(): pl.pallas_call(forward_kernel, grid=(total // block,), in_specs=[by_row,...]
    reduce_sum x1 -> x4, other arithmetic: 50.7 us -> 0.92 us  [the longest x1 0.3 us: shards(): t_total = jnp.sum(t_sum * t_scale, axis=0)]
    convert_element_type x2 -> x5, other arithmetic: 54.2 us -> 4.99 us  [the longest x1 3.25 us: shards(): (s_wide * t_factor).astype(bf16)]
    all_gather x5 -> x0, blocking collectives: 40 us -> none  [joined(): pieces = jax.tree.map(lambda part: lax.all_gather(part, axis), value)]
  transfers between devices with their start and end apart: 3 -> 3, of which waited for: 2 -> 3; matrix products, arithmetic and copies ran while one was open for 21% -> 6% of each run, Pallas kernels for 0% -> 5%
where the time goes in v1:
time: 334 us; the launch traced here: 333 us
  waiting for transfers between devices  207 us (62%)
  Pallas kernels  63.5 us (19%)
  between operations  22 us (7%)
  other arithmetic  15.2 us (5%)
  local copies, waits for them, and re-layouts  13.7 us (4%)
  matrix products  11.9 us (4%)
    psum x1, waiting for transfers between devices, shards(): d_all = lax.psum(d_part, ('dp', 'proto'))  111 us
    all_gather x1, waiting for transfers between devices, shards(): everyone = lax.all_gather(sent, ('dp', 'proto'))  59.7 us
    pallas_call x1, Pallas kernels, forward(): pl.pallas_call(forward_kernel, grid=(total // block,), in_specs=[by_row,...  38.5 us
    all_gather x1, waiting for transfers between devices, shards(): all_stats = lax.all_gather(stats[:5], ('dp', 'proto'))  36 us
    pallas_call x1, Pallas kernels, proto_grad_call(): pl.pallas_call(proto_grad_kernel, grid=(cols // block,), in_specs=[tall,...  18 us
    dot_general x1, matrix products, shards(): jnp.dot(parts, prototypes, preferred_element_type=f32)  8.73 us
    pallas_call x1, Pallas kernels, compact(): pl.pallas_call(functools.partial(compact_kernel, max_masked), out_shape=[...  7.06 us
  transfers between devices with their start and end apart: 3, of which 3 were waited for; matrix products, arithmetic and copies ran while one was open for 6% of the time, Pallas kernels for 5%

profile of v1, /device:TPU:0, one launch (start us, length us, event | category | flops | bytes accessed | tf_op | source)
XLA Modules:
  0.0 333.3 jit_solution(2788845115281611463)
XLA Ops:
  7.2 1.6 fusion.2
  9.3 0.7 fusion.26
  10.1 1.7 fusion.56
  11.8 2.5 copy.34.pt_ref
  14.2 0.7 dynamic-slice_multiply_fusion
  15.0 3.1 constant_dynamic-slice_fusion.p_ref
  18.1 59.7 %all-gather.6.cloned.1.call-done = bf16[4608,512]{1,0:T(8,128)(2,1)} async-done(((bf16[144,512]{1,0:T(8,128)(2,1)}), bf16[4608,512]{1,0:T(8,128)(2,1)}) %all-gather.6.cloned.1.call-update) | async-done | bytes 4718608 | tf_op jit(solution)/shard_map/all_gather | solution.py:216
  77.8 0.7 fusion.50
  78.5 0.7 slice_convert_fusion
  80.1 7.1 %compact_rows.1 = (bf16[2048,256]{1,0:T(8,128)(2,1)}, bf16[2048,256]{1,0:T(8,128)(2,1)}) custom-call(s32[32]{0:T(128)} %sub.66.starts_ref, bf16[32,144,512]{2,1,0:T(8,128)(2,1)} %bitcast.63), custom_call_target="tpu_custom_call" | custom-call | tf_op jit(solution)/shard_map/compact_rows/pallas_call | solution.py:58
  87.1 1.9 broadcast_in_dim.19.c_ref
  89.0 38.5 %forward_rows.1 = (bf16[4096,2048]{1,0:T(8,128)(2,1)}, bf16[4096,2048]{1,0:T(8,128)(2,1)}, f32[2048,256]{1,0:T(8,128)}, f32[2048,256]{1,0:T(8,128)}, f32[8,2048]{1,0:T(8,128)}) custom-call(bf16[2048,256]{1,0:T(8,128)(2,1)} %get-tuple-element.11.s_ref, bf16[2048,256]{1,0:T(8,128)(2,1)} %get-tuple-element.12.t_ref, bf16[4096,256]{1,0:T(8,128)(2,1)} %copy.34.pt_ref, ...), custom_call_target="tpu_custom_call" | custom-call | flops 17179869184 | bytes 33554432 | tf_op jit(solution)/shard_map/forward_rows/pallas_call | solution.py:142
  127.5 1.5 slice_bitcast_fusion
  130.1 0.7 fusion.53
  138.6 0.9 fusion.52
  139.6 8.7 %convolution_reduce_fusion = f32[32768]{0:T(1024)} fusion(bf16[256,32768]{1,0:T(8,128)(2,1)} %param.9, bf16[1,256]{1,0:T(2,128)(2,1)S(1)} %get-tuple-element.44, bf16[1,256]{1,0:T(2,128)(2,1)S(1)} %get-tuple-element.45, bf16[1,256]{1,0:T(2,128)(2,1)S(1)} %get-tuple-element.43), kind=kOutput, calls=%fused_computation.6 | convolution fusion | flops 134467584 | bytes 16909824 | tf_op jit(solution)/shard_map/dot_general | solution.py:258
  148.3 36.0 %all-gather.8.cloned.1.call-done = f32[32,5,2048]{2,1,0:T(8,128)} async-done(((f32[1,5,2048]{2,1,0:T(8,128)}), f32[32,5,2048]{2,1,0:T(8,128)}) %all-gather.8.cloned.1.call-update) | async-done | bytes 1310736 | tf_op jit(solution)/shard_map/all_gather | solution.py:232
  184.4 5.9 %slice_reduce_fusion.1 = (f32[2048]{0:T(1024)S(1)}, f32[2048]{0:T(1024)S(1)}, f32[32,1,2048]{2,1,0:T(1,128)S(1)}, f32[32,1,2048]{2,1,0:T(1,128)S(1)}, f32[32,1,2...) fusion(f32[32,5,2048]{2,1,0:T(8,128)} %all-gather.8.cloned.1.call-done), kind=kLoop, calls=%fused_computation.95 | loop fusion | flops 126976 | bytes 2637824 | tf_op jit(solution)/shard_map/reduce_max | solution.py:235
  190.8 0.6 multiply_divide_fusion.1
  191.4 3.2 fusion.1
  194.7 18.0 %proto_grad_rows.1 = f32[4096,256]{1,0:T(8,128)} custom-call(bf16[4096,2048]{1,0:T(8,128)(2,1)} %get-tuple-element.16.us_ref, bf16[4096,2048]{1,0:T(8,128)(2,1)} %get-tuple-element.17.ut_ref, bf16[2048,256]{1,0:T(8,128)(2,1)} %get-tuple-element.30.s_ref, bf16[2048,256]{1,0:T(8,128)(2,1)} %get-tuple-element.29.t_ref), custom_call_target="tpu_custom_call" | custom-call | flops 8589934592 | bytes 33554432 | tf_op jit(solution)/shard_map/proto_grad_rows/pallas_call | solution.py:177
  212.7 110.8 %all-reduce.5.cloned.1.call-done = bf16[2048,256]{1,0:T(8,128)(2,1)} async-done(((bf16[2048,256]{1,0:T(8,128)(2,1)}), bf16[2048,256]{1,0:T(8,128)(2,1)}) %all-reduce.5.cloned.1.call-update) | async-done | bytes 1048592 | tf_op jit(solution)/shard_map/psum | solution.py:247
  323.5 1.2 pad_dynamic-slice_fusion.3
  325.1 1.6 fusion.10
  (39 shorter events, 3.2 us)
Async XLA Ops:
  7.2 1.9 copy-start.5
  7.2 70.6 %all-gather.6.cloned.1.call-start = ((), (), s32[]{:S(2)}) async-start(), calls=%async_computation.1 | async-start | bytes 4866048 | tf_op jit(solution)/shard_map/all_gather | solution.py:216
  10.0 174.4 %all-gather.8.cloned.1.call-start = ((), (), s32[]{:S(2)}) async-start(), calls=%async_computation.2 | async-start | bytes 2162688 | tf_op jit(solution)/shard_map/all_gather | solution.py:232
  89.0 40.9 %copy-start.4 = (s32[32]{0:T(128)S(1)}, s32[32]{0:T(128)}, u32[]{:S(2)}) copy-start(s32[32]{0:T(128)} %sub.66.starts_ref) | copy-start | bytes 388
  89.0 49.3 %copy-start.1 = (bf16[2048,256]{1,0:T(8,128)(2,1)S(1)}, bf16[2048,256]{1,0:T(8,128)(2,1)}, u32[]{:S(2)}) copy-start(bf16[2048,256]{1,0:T(8,128)(2,1)} %get-tuple-element.12.t_ref) | copy-start | bytes 3145732
  129.0 194.5 %all-reduce.5.cloned.1.call-start = ((), (), s32[]{:S(2)}) async-start(), calls=%async_computation | async-start | bytes 2097152 | tf_op jit(solution)/shard_map/psum | solution.py:247
  148.3 43.1 %copy-start = (f32[2048,256]{1,0:T(8,128)S(1)}, f32[2048,256]{1,0:T(8,128)}, u32[]{:S(2)}) copy-start(f32[2048,256]{1,0:T(8,128)} %get-tuple-element.14) | copy-start | bytes 6291460
  184.4 7.0 %copy-start.2 = (bf16[2048,256]{1,0:T(8,128)(2,1)S(1)}, bf16[2048,256]{1,0:T(8,128)(2,1)}, u32[]{:S(2)}) copy-start(bf16[2048,256]{1,0:T(8,128)(2,1)} %get-tuple-element.11.s_ref) | copy-start | bytes 3145732
  212.7 112.5 %copy-start.3 = (s32[4,128]{1,0:T(4,128)S(1)}, s32[4,128]{1,0:T(4,128)}, u32[]{:S(2)}) copy-start(s32[4,128]{1,0:T(4,128)} %param.11) | copy-start | bytes 6148
Sparse Core Ops, SparseCore 0:
  11.5 66.2 all-gather.5
  129.1 55.1 all-gather.7
  194.8 128.6 all-reduce.4

commit v2 on v1

--- a/solution.py
+++ b/solution.py
@@ -67,6 +67,48 @@
         compiler_params=pltpu.CompilerParams(vmem_limit_bytes=vmem_bytes),
         name="compact_rows",
     )(starts, rows)
+
+
+def expand_kernel(max_masked, starts_ref, rows_ref, out_ref):
+    tall = max_masked + 8
+
+    @pl.loop(0, out_ref.shape[0] // max_masked)
+    def _(image):
+        at = starts_ref[image]
+        base = pl.multiple_of(at // 8 * 8, 8)
+        ahead = at - base
+        value = rows_ref[pl.ds(base, tall), :]
+        value = pltpu.roll(value, jnp.where(ahead == 0, 0, tall - ahead), 0)
+        to = pl.multiple_of(image * max_masked, max_masked)
+        out_ref[pl.ds(to, max_masked), :] = value[:max_masked].astype(bf16)
+
+
+def expand(rows, starts, max_masked):
+    return pl.pallas_call(
+        functools.partial(expand_kernel, max_masked),
+        out_shape=jax.ShapeDtypeStruct((starts.shape[0] * max_masked, rows.shape[1]), bf16),
+        in_specs=[
+            pl.BlockSpec(memory_space=pltpu.SMEM),
+            pl.BlockSpec(memory_space=pltpu.VMEM),
+        ],
+        out_specs=pl.BlockSpec(memory_space=pltpu.VMEM),
+        compiler_params=pltpu.CompilerParams(vmem_limit_bytes=vmem_bytes),
+        name="expand_rows",
+    )(starts, rows)
+
+
+def merge_stats(stats):
+    t_top, t_sum, cross, s_top, s_sum = (stats[:, k] for k in range(5))
+    t_all = jnp.max(t_top, axis=0)
+    s_all = jnp.max(s_top, axis=0)
+    t_scale = jnp.exp2(t_top - t_all)
+    return (
+        t_all,
+        jnp.sum(t_sum * t_scale, axis=0),
+        jnp.sum(cross * t_scale, axis=0),
+        s_all,
+        jnp.sum(s_sum * jnp.exp2(s_top - s_all), axis=0),
+    )
 
 
 def nt_dot(left, right):
@@ -192,14 +234,11 @@
     img_local, patches, width = student_rows.shape
     max_masked = mask_index.shape[1]
     data_size = lax.axis_size("dp")
-    proto_size = lax.axis_size("proto")
     me_data = lax.axis_index("dp")
-    me_proto = lax.axis_index("proto")
     images = img_local * data_size
     padded_rows = img_local * max_masked
     total = images * max_masked // 2
     cols = prototypes.shape[1] // data_size
-    piece = padded_rows // proto_size
 
     patch_ids = jnp.arange(patches, dtype=jnp.int32)
     pick = (mask_index[:, :, None] == patch_ids).astype(bf16)
@@ -210,11 +249,10 @@
     t_unit, _ = unit_rows(picked[:, width:])
     halves = jnp.concatenate([s_unit.astype(bf16), t_unit.astype(bf16)], axis=1)
 
-    mine = lax.dynamic_slice_in_dim(halves, me_proto * piece, piece, axis=0)
     counts_row = jnp.pad(mask_count.astype(bf16)[None, :], ((0, tail_rows - 1), (0, 2 * width - img_local)))
-    sent = jnp.concatenate([mine, counts_row], axis=0)
-    everyone = lax.all_gather(sent, ("dp", "proto"))
-    counts = everyone[::proto_size, piece, :img_local].astype(jnp.int32).reshape(images)
+    sent = jnp.concatenate([halves, counts_row], axis=0)
+    everyone = lax.all_gather(sent, "dp")
+    counts = everyone[:, padded_rows, :img_local].astype(jnp.int32).reshape(images)
     ends = jnp.cumsum(counts)
     starts = ends - counts
     s_half, t_half = compact(everyone, starts, max_masked, total, width)
@@ -229,22 +267,18 @@
     shift = jnp.broadcast_to((my_center * (log2_e / teacher_temp))[:, None], (cols, 128))
     us, ut, s_acc, t_acc, stats = forward(s_half, t_half, protos.T, protos, shift)
 
-    all_stats = lax.all_gather(stats[:5], ("dp", "proto"))
-    t_top, t_sum, cross, s_top, s_sum = (all_stats[:, k] for k in range(5))
-    t_all = jnp.max(t_top, axis=0)
-    s_all = jnp.max(s_top, axis=0)
-    t_scale = jnp.exp2(t_top - t_all)
-    t_total = jnp.sum(t_sum * t_scale, axis=0)
-    s_total = jnp.sum(s_sum * jnp.exp2(s_top - s_all), axis=0)
-    cross_mean = jnp.sum(cross * t_scale, axis=0) / t_total
+    merged = merge_stats(lax.all_gather(stats[:5], "proto"))
+    t_all, t_total, cross, s_all, s_total = merge_stats(lax.all_gather(jnp.stack(merged), "dp"))
+    cross_mean = cross / t_total
     ce = ln_2 * (s_all + jnp.log2(s_total)) - cross_mean / student_temp
     loss = jnp.sum(weight * ce)
 
     coef = loss_scale * weight / student_temp
     s_factor = (coef * jnp.exp2(stats[3] - s_all) / s_total)[:, None]
     t_factor = (coef * jnp.exp2(stats[0] - t_all) / t_total)[:, None]
-    d_part = (s_factor * s_acc - t_factor * t_acc).astype(bf16)
-    d_all = lax.psum(d_part, ("dp", "proto"))
+    d_part = jnp.pad(s_factor * s_acc - t_factor * t_acc, ((0, max_masked + 8), (0, 0)))
+    d_slots = expand(d_part, starts, max_masked)
+    d_mine = lax.psum_scatter(d_slots, "dp", scatter_dimension=0, tiled=True)
 
     s_wide = s_half.astype(f32)
     proto_grad = proto_grad_call(us, ut, (s_wide * s_factor).astype(bf16), (s_wide * t_factor).astype(bf16))
@@ -257,11 +291,7 @@
     parts = jnp.pad(parts, ((0, 5), (0, 0)))
     patch_center = jnp.sum(jnp.dot(parts, prototypes, preferred_element_type=f32), axis=0)
 
-    d_all = jnp.pad(d_all, ((0, max_masked), (0, 0)))
-    my_starts = lax.dynamic_slice_in_dim(starts, me_data * img_local, img_local)
-    d_unit = jnp.concatenate(
-        [lax.dynamic_slice_in_dim(d_all, my_starts[i], max_masked, axis=0) for i in range(img_local)]
-    ).astype(f32)
+    d_unit = lax.psum(d_mine, "proto").astype(f32)
     row_grads = norm_backward(d_unit, s_unit, s_len).reshape(img_local, max_masked, width)
     slots = jnp.arange(max_masked, dtype=jnp.int32)
     valid = slots[None, :] < mask_count[:, None]

time: 334 us -> 237 us (0.71)
  waiting for transfers between devices: 207 us -> 92.5 us
  blocking collectives: 0 us -> 23.8 us
  between operations: 22 us -> 14.6 us
  Pallas kernels: 63.5 us -> 68 us
  other arithmetic: 15.2 us -> 11.6 us
    psum x1, waiting for transfers between devices: 111 us -> 26.4 us  [shards(): d_unit = lax.psum(d_mine, 'proto').astype(f32)]
    all_gather x2 -> x1, waiting for transfers between devices: 95.7 us -> 42.6 us  [shards(): everyone = lax.all_gather(sent, 'dp')]
    all_gather x0 -> x2, blocking collectives: none -> 23.8 us  [the longest x1 14.8 us: shards(): lax.all_gather(jnp.stack(merged), 'dp')]
    reduce_scatter x0 -> x1, waiting for transfers between devices: none -> 23.4 us  [shards(): d_mine = lax.psum_scatter(d_slots, 'dp', scatter_dimension=0, tiled=True)]
    reduce_max x1 -> x2, other arithmetic: 5.89 us -> 0.45 us  [merge_stats(): s_all = jnp.max(s_top, axis=0)]
    pallas_call x0 -> x1, Pallas kernels: none -> 4.71 us  [expand(): pl.pallas_call(functools.partial(expand_kernel, max_masked), out_shape=ja...]
  transfers between devices with their start and end apart: 3 -> 3, of which waited for: 3 -> 3; matrix products, arithmetic and copies ran while one was open for 6% -> 7% of each run, Pallas kernels for 5% -> 8%
where the time goes in v2:
time: 237 us
  waiting for transfers between devices  92.5 us (39%)
  Pallas kernels  68 us (29%)
  blocking collectives  23.8 us (10%)
  between operations  14.6 us (6%)
  local copies, waits for them, and re-layouts  13.8 us (6%)
  matrix products  12.1 us (5%)
  other arithmetic  11.6 us (5%)
    all_gather x1, waiting for transfers between devices, shards(): everyone = lax.all_gather(sent, 'dp')  42.6 us
    pallas_call x1, Pallas kernels, forward(): pl.pallas_call(forward_kernel, grid=(total // block,), in_specs=[by_row,...  38.4 us
    psum x1, waiting for transfers between devices, shards(): d_unit = lax.psum(d_mine, 'proto').astype(f32)  26.4 us
    reduce_scatter x1, waiting for transfers between devices, shards(): d_mine = lax.psum_scatter(d_slots, 'dp', scatter_dimension=0, tiled=True)  23.4 us
    pallas_call x1, Pallas kernels, proto_grad_call(): pl.pallas_call(proto_grad_kernel, grid=(cols // block,), in_specs=[tall,...  18 us
    all_gather x1, blocking collectives, shards(): lax.all_gather(jnp.stack(merged), 'dp')  14.8 us
    all_gather x1, blocking collectives, shards(): merged = merge_stats(lax.all_gather(stats[:5], 'proto'))  8.97 us
    dot_general x1, matrix products, shards(): jnp.dot(parts, prototypes, preferred_element_type=f32)  8.93 us
  transfers between devices with their start and end apart: 3, of which 3 were waited for; matrix products, arithmetic and copies ran while one was open for 7% of the time, Pallas kernels for 8%

profile of v2, /device:TPU:0, one launch (start us, length us, event | category | flops | bytes accessed | tf_op | source)
XLA Modules:
  0.0 236.6 jit_solution(9146505088659988494)
XLA Ops:
  7.2 1.6 fusion.3
  9.3 0.8 fusion.7
  10.2 1.7 fusion.65
  11.9 2.5 %copy.46.pt_ref = bf16[4096,256]{1,0:T(8,128)(2,1)} copy(bf16[4096,256]{0,1:T(8,128)(2,1)S(1)} %fusion.65) | data formatting | bytes 4194304 | tf_op jit(solution)/shard_map/transpose | solution.py:268
  15.8 3.1 %constant_dynamic-slice_fusion.p_ref = bf16[256,4096]{1,0:T(8,128)(2,1)} fusion(bf16[256,32768]{1,0:T(8,128)(2,1)} %param.9, s32[]{:T(128)S(6)} %select_n.9), kind=kLoop, calls=%fused_computation.95 | loop fusion | bytes 4194308 | tf_op jit(solution)/shard_map/dynamic_slice | solution.py:265
  18.9 42.6 %all-gather.7.cloned.1.call-done = bf16[4224,512]{1,0:T(8,128)(2,1)} async-done(((bf16[528,512]{1,0:T(8,128)(2,1)}), bf16[4224,512]{1,0:T(8,128)(2,1)}) %all-gather.7.cloned.1.call-update) | async-done | bytes 4325392 | tf_op jit(solution)/shard_map/all_gather | solution.py:254
  63.8 7.0 %compact_rows.1 = (bf16[2048,256]{1,0:T(8,128)(2,1)}, bf16[2048,256]{1,0:T(8,128)(2,1)}) custom-call(s32[32]{0:T(128)} %sub.82.starts_ref, bf16[8,528,512]{2,1,0:T(8,128)(2,1)} %bitcast.103), custom_call_target="tpu_custom_call" | custom-call | tf_op jit(solution)/shard_map/compact_rows/pallas_call | solution.py:58
  70.7 1.9 broadcast_in_dim.19.c_ref
  72.6 38.4 %forward_rows.1 = (bf16[4096,2048]{1,0:T(8,128)(2,1)}, bf16[4096,2048]{1,0:T(8,128)(2,1)}, f32[2048,256]{1,0:T(8,128)}, f32[2048,256]{1,0:T(8,128)}, f32[8,2048]{1,0:T(8,128)}) custom-call(bf16[2048,256]{1,0:T(8,128)(2,1)} %get-tuple-element.11.s_ref, bf16[2048,256]{1,0:T(8,128)(2,1)} %get-tuple-element.12.t_ref, bf16[4096,256]{1,0:T(8,128)(2,1)} %copy.46.pt_ref, ...), custom_call_target="tpu_custom_call" | custom-call | flops 17179869184 | bytes 33554432 | tf_op jit(solution)/shard_map/forward_rows/pallas_call | solution.py:184
  111.0 1.0 slice_bitcast_fusion
  112.0 0.9 fusion.62
  112.9 9.0 %all-gather.3 = f32[4,5,2048]{2,1,0:T(8,128)S(1)} all-gather(f32[1,5,2048]{2,1,0:T(8,128)S(1)} %slice_bitcast_fusion), channel_id=3, replica_groups=mesh['dp'=8,'proto'=4] {'proto'}, dimensions={0}, use_global_device_ids=true | all-gather | bytes 204800 | tf_op jit(solution)/shard_map/all_gather | solution.py:270
  122.3 14.8 %all-gather.4 = f32[8,5,2048]{2,1,0:T(8,128)S(1)} all-gather(f32[1,5,2048]{2,1,0:T(8,128)S(1)} %bitcast.105), channel_id=4, replica_groups=mesh['dp'=8,'proto'=4] {'dp'}, dimensions={0}, use_global_device_ids=true | all-gather | bytes 368640 | tf_op jit(solution)/shard_map/all_gather | solution.py:271
  138.4 3.2 %fusion.1 = (bf16[2048,256]{1,0:T(8,128)(2,1)}, bf16[2048,256]{1,0:T(8,128)(2,1)}, f32[2048,256]{1,0:T(8,128)S(1)}) fusion(bf16[2048,256]{1,0:T(8,128)(2,1)} %get-tuple-element.11.s_ref, f32[2048]{0:T(1024)S(1)} %get-tuple-element.46, f32[2048]{0:T(1024)S(1)} %get-tuple-element.44, f32[2048,256]{1,0:T(8,128)} %get-tuple-element.15, f32[2048,256]{1,0:T(8,128)S(1)} %copy-done), kind=kLoop, calls=%fused_computation.3 | loop fusion | flops 4194304 | bytes 9453568 | tf_op jit(solution)/shard_map/convert_element_type | solution.py:284
  141.6 1.5 pad.13.rows_ref
  143.1 4.7 %expand_rows.1 = bf16[4096,256]{1,0:T(8,128)(2,1)} custom-call(s32[32]{0:T(128)} %sub.82.starts_ref, f32[2184,256]{1,0:T(8,128)} %pad.13.rows_ref), custom_call_target="tpu_custom_call" | custom-call | tf_op jit(solution)/shard_map/expand_rows/pallas_call | solution.py:87
  148.1 0.9 copy-done.1
  149.3 8.9 %convolution_reduce_fusion = f32[32768]{0:T(1024)} fusion(bf16[256,32768]{1,0:T(8,128)(2,1)} %param.9, bf16[1,256]{1,0:T(2,128)(2,1)S(1)} %get-tuple-element.49, bf16[1,256]{1,0:T(2,128)(2,1)S(1)} %get-tuple-element.50, bf16[1,256]{1,0:T(2,128)(2,1)S(1)} %get-tuple-element.48), kind=kOutput, calls=%fused_computation.6 | convolution fusion | flops 134467584 | bytes 16909824 | tf_op jit(solution)/shard_map/dot_general | solution.py:292
  158.2 23.4 %reduce-scatter.2.cloned.1.call-done = bf16[512,256]{1,0:T(8,128)(2,1)} async-done(((bf16[4096,256]{1,0:T(8,128)(2,1)}), bf16[512,256]{1,0:T(8,128)(2,1)}) %reduce-scatter.2.cloned.1.call-update) | async-done | bytes 262160 | tf_op jit(solution)/shard_map/reduce_scatter | solution.py:281
  181.7 18.0 %proto_grad_rows.1 = f32[4096,256]{1,0:T(8,128)} custom-call(bf16[4096,2048]{1,0:T(8,128)(2,1)} %get-tuple-element.16.us_ref, bf16[4096,2048]{1,0:T(8,128)(2,1)} %get-tuple-element.17.ut_ref, bf16[2048,256]{1,0:T(8,128)(2,1)} %get-tuple-element.29.s_ref, bf16[2048,256]{1,0:T(8,128)(2,1)} %get-tuple-element.28.t_ref), custom_call_target="tpu_custom_call" | custom-call | flops 8589934592 | bytes 33554432 | tf_op jit(solution)/shard_map/proto_grad_rows/pallas_call | solution.py:219
  199.7 26.4 %all-reduce.5.cloned.1.call-done = bf16[512,256]{1,0:T(8,128)(2,1)} async-done(((bf16[512,256]{1,0:T(8,128)(2,1)}), bf16[512,256]{1,0:T(8,128)(2,1)}) %all-reduce.5.cloned.1.call-update) | async-done | bytes 262160 | tf_op jit(solution)/shard_map/psum | solution.py:294
  226.2 1.2 fusion.8
  227.3 1.2 fusion.9
  228.5 1.6 fusion.11
  (41 shorter events, 5.8 us)
Async XLA Ops:
  7.2 1.8 copy-start.4
  7.2 54.3 %all-gather.7.cloned.1.call-start = ((), (), s32[]{:S(2)}) async-start(), calls=%async_computation.3 | async-start | bytes 4866048 | tf_op jit(solution)/shard_map/all_gather | solution.py:254
  10.1 171.6 %reduce-scatter.2.cloned.1.call-start = ((), (), s32[]{:S(2)}) async-start(), calls=%async_computation.1 | async-start | bytes 2359296 | tf_op jit(solution)/shard_map/reduce_scatter | solution.py:281
  111.0 26.4 %copy-start.3 = (s32[32]{0:T(128)S(1)}, s32[32]{0:T(128)}, u32[]{:S(2)}) copy-start(s32[32]{0:T(128)} %sub.82.starts_ref) | copy-start | bytes 388
  111.0 27.4 %copy-start = (f32[2048,256]{1,0:T(8,128)S(1)}, f32[2048,256]{1,0:T(8,128)}, u32[]{:S(2)}) copy-start(f32[2048,256]{1,0:T(8,128)} %get-tuple-element.14) | copy-start | bytes 6291460
  147.8 1.2 copy-start.1
  147.8 78.3 %all-reduce.5.cloned.1.call-start = ((), (), s32[]{:S(2)}) async-start(), calls=%async_computation.2 | async-start | bytes 524288 | tf_op jit(solution)/shard_map/psum | solution.py:294
  199.7 28.8 %copy-start.2 = (s32[4,128]{1,0:T(4,128)S(1)}, s32[4,128]{1,0:T(4,128)}, u32[]{:S(2)}) copy-start(s32[4,128]{1,0:T(4,128)} %param.11) | copy-start | bytes 6148
Sparse Core Ops, SparseCore 0:
  10.2 51.1 all-gather.6
  147.9 33.7 reduce-scatter.1
  184.6 41.4 all-reduce.4

commit v3 on v2

--- a/solution.py
+++ b/solution.py
@@ -291,7 +291,7 @@
     parts = jnp.pad(parts, ((0, 5), (0, 0)))
     patch_center = jnp.sum(jnp.dot(parts, prototypes, preferred_element_type=f32), axis=0)
 
-    d_unit = lax.psum(d_mine, "proto").astype(f32)
+    d_unit = lax.psum(d_mine.astype(f32), "proto")
     row_grads = norm_backward(d_unit, s_unit, s_len).reshape(img_local, max_masked, width)
     slots = jnp.arange(max_masked, dtype=jnp.int32)
     valid = slots[None, :] < mask_count[:, None]

time: 237 us -> 216 us (0.911)
  waiting for transfers between devices: 92.5 us -> 47.9 us
  blocking collectives: 23.8 us -> 48.7 us
    psum x1 -> x0, waiting for transfers between devices: 26.4 us -> none  [shards(): d_unit = lax.psum(d_mine, 'proto').astype(f32)]
    psum x0 -> x1, blocking collectives: none -> 24.7 us  [shards(): d_unit = lax.psum(d_mine.astype(f32), 'proto')]
    reduce_scatter x1, waiting for transfers between devices: 23.4 us -> 5.35 us  [shards(): d_mine = lax.psum_scatter(d_slots, 'dp', scatter_dimension=0, tiled=True)]
  transfers between devices with their start and end apart: 3 -> 2, of which waited for: 3 -> 2; matrix products, arithmetic and copies ran while one was open for 7% -> 8% of each run, Pallas kernels for 8% -> 8%
where the time goes in v3:
time: 216 us; the launch traced here: 215 us
  Pallas kernels  68.2 us (32%)
  blocking collectives  48.7 us (23%)
  waiting for transfers between devices  47.9 us (22%)
  between operations  14.9 us (7%)
  local copies, waits for them, and re-layouts  14 us (6%)
  matrix products  12 us (6%)
  other arithmetic  9.67 us (4%)
    all_gather x1, waiting for transfers between devices, shards(): everyone = lax.all_gather(sent, 'dp')  42.6 us
    pallas_call x1, Pallas kernels, forward(): pl.pallas_call(forward_kernel, grid=(total // block,), in_specs=[by_row,...  38.4 us
    psum x1, blocking collectives, shards(): d_unit = lax.psum(d_mine.astype(f32), 'proto')  24.7 us
    pallas_call x1, Pallas kernels, proto_grad_call(): pl.pallas_call(proto_grad_kernel, grid=(cols // block,), in_specs=[tall,...  18.2 us
    all_gather x1, blocking collectives, shards(): lax.all_gather(jnp.stack(merged), 'dp')  15 us
    all_gather x1, blocking collectives, shards(): merged = merge_stats(lax.all_gather(stats[:5], 'proto'))  8.97 us
    dot_general x1, matrix products, shards(): jnp.dot(parts, prototypes, preferred_element_type=f32)  8.84 us
    pallas_call x1, Pallas kernels, compact(): pl.pallas_call(functools.partial(compact_kernel, max_masked), out_shape=[...  6.97 us
  transfers between devices with their start and end apart: 2, of which 2 were waited for; matrix products, arithmetic and copies ran while one was open for 8% of the time, Pallas kernels for 8%

profile of v3, /device:TPU:0, one launch (start us, length us, event | category | flops | bytes accessed | tf_op | source)
XLA Modules:
  0.0 215.5 jit_solution(15692402724863099713)
XLA Ops:
  7.2 1.6 fusion.3
  9.3 0.8 fusion.7
  10.2 1.7 fusion.63
  11.9 2.5 %copy.46.pt_ref = bf16[4096,256]{1,0:T(8,128)(2,1)} copy(bf16[4096,256]{0,1:T(8,128)(2,1)S(1)} %fusion.63) | data formatting | bytes 4194304 | tf_op jit(solution)/shard_map/transpose | solution.py:268
  15.0 0.7 dynamic-slice_multiply_fusion
  15.8 3.1 %constant_dynamic-slice_fusion.p_ref = bf16[256,4096]{1,0:T(8,128)(2,1)} fusion(bf16[256,32768]{1,0:T(8,128)(2,1)} %param.9, s32[]{:T(128)S(6)} %select_n.9), kind=kLoop, calls=%fused_computation.93 | loop fusion | bytes 4194308 | tf_op jit(solution)/shard_map/dynamic_slice | solution.py:265
  18.9 42.6 %all-gather.7.cloned.1.call-done = bf16[4224,512]{1,0:T(8,128)(2,1)} async-done(((bf16[528,512]{1,0:T(8,128)(2,1)}), bf16[4224,512]{1,0:T(8,128)(2,1)}) %all-gather.7.cloned.1.call-update) | async-done | bytes 4325392 | tf_op jit(solution)/shard_map/all_gather | solution.py:254
  61.4 0.7 fusion.58
  63.8 7.0 %compact_rows.1 = (bf16[2048,256]{1,0:T(8,128)(2,1)}, bf16[2048,256]{1,0:T(8,128)(2,1)}) custom-call(s32[32]{0:T(128)} %sub.82.starts_ref, bf16[8,528,512]{2,1,0:T(8,128)(2,1)} %bitcast.103), custom_call_target="tpu_custom_call" | custom-call | tf_op jit(solution)/shard_map/compact_rows/pallas_call | solution.py:58
  70.7 1.9 broadcast_in_dim.19.c_ref
  72.6 38.4 %forward_rows.1 = (bf16[4096,2048]{1,0:T(8,128)(2,1)}, bf16[4096,2048]{1,0:T(8,128)(2,1)}, f32[2048,256]{1,0:T(8,128)}, f32[2048,256]{1,0:T(8,128)}, f32[8,2048]{1,0:T(8,128)}) custom-call(bf16[2048,256]{1,0:T(8,128)(2,1)} %get-tuple-element.11.s_ref, bf16[2048,256]{1,0:T(8,128)(2,1)} %get-tuple-element.12.t_ref, bf16[4096,256]{1,0:T(8,128)(2,1)} %copy.46.pt_ref, ...), custom_call_target="tpu_custom_call" | custom-call | flops 17179869184 | bytes 33554432 | tf_op jit(solution)/shard_map/forward_rows/pallas_call | solution.py:184
  111.0 1.0 slice_bitcast_fusion
  112.0 0.9 fusion.60
  112.9 9.0 %all-gather.3 = f32[4,5,2048]{2,1,0:T(8,128)S(1)} all-gather(f32[1,5,2048]{2,1,0:T(8,128)S(1)} %slice_bitcast_fusion), channel_id=3, replica_groups=mesh['dp'=8,'proto'=4] {'proto'}, dimensions={0}, use_global_device_ids=true | all-gather | bytes 204800 | tf_op jit(solution)/shard_map/all_gather | solution.py:270
  122.3 15.0 %all-gather.4 = f32[8,5,2048]{2,1,0:T(8,128)S(1)} all-gather(f32[1,5,2048]{2,1,0:T(8,128)S(1)} %bitcast.105), channel_id=4, replica_groups=mesh['dp'=8,'proto'=4] {'dp'}, dimensions={0}, use_global_device_ids=true | all-gather | bytes 368640 | tf_op jit(solution)/shard_map/all_gather | solution.py:271
  138.6 3.2 %fusion.1 = (bf16[2048,256]{1,0:T(8,128)(2,1)}, bf16[2048,256]{1,0:T(8,128)(2,1)}, f32[2048,256]{1,0:T(8,128)S(1)}) fusion(bf16[2048,256]{1,0:T(8,128)(2,1)} %get-tuple-element.11.s_ref, f32[2048]{0:T(1024)S(1)} %get-tuple-element.46, f32[2048]{0:T(1024)S(1)} %get-tuple-element.44, f32[2048,256]{1,0:T(8,128)} %get-tuple-element.15, f32[2048,256]{1,0:T(8,128)S(1)} %copy-done), kind=kLoop, calls=%fused_computation.3 | loop fusion | flops 4194304 | bytes 9453568 | tf_op jit(solution)/shard_map/convert_element_type | solution.py:284
  141.7 1.5 pad.13.rows_ref
  143.3 4.7 %expand_rows.1 = bf16[4096,256]{1,0:T(8,128)(2,1)} custom-call(s32[32]{0:T(128)} %sub.82.starts_ref, f32[2184,256]{1,0:T(8,128)} %pad.13.rows_ref), custom_call_target="tpu_custom_call" | custom-call | tf_op jit(solution)/shard_map/expand_rows/pallas_call | solution.py:87
  148.1 1.1 copy-done.1
  149.5 18.2 %proto_grad_rows.1 = f32[4096,256]{1,0:T(8,128)} custom-call(bf16[4096,2048]{1,0:T(8,128)(2,1)} %get-tuple-element.16.us_ref, bf16[4096,2048]{1,0:T(8,128)(2,1)} %get-tuple-element.17.ut_ref, bf16[2048,256]{1,0:T(8,128)(2,1)} %get-tuple-element.29.s_ref, bf16[2048,256]{1,0:T(8,128)(2,1)} %get-tuple-element.28.t_ref), custom_call_target="tpu_custom_call" | custom-call | flops 8589934592 | bytes 33554432 | tf_op jit(solution)/shard_map/proto_grad_rows/pallas_call | solution.py:219
  167.7 8.8 %convolution_reduce_fusion = f32[32768]{0:T(1024)} fusion(bf16[256,32768]{1,0:T(8,128)(2,1)} %param.9, bf16[1,256]{1,0:T(2,128)(2,1)S(1)} %get-tuple-element.49, bf16[1,256]{1,0:T(2,128)(2,1)S(1)} %get-tuple-element.50, bf16[1,256]{1,0:T(2,128)(2,1)S(1)} %get-tuple-element.48), kind=kOutput, calls=%fused_computation.6 | convolution fusion | flops 134467584 | bytes 16909824 | tf_op jit(solution)/shard_map/dot_general | solution.py:292
  176.5 5.4 %reduce-scatter.2.cloned.1.call-done = bf16[512,256]{1,0:T(8,128)(2,1)} async-done(((bf16[4096,256]{1,0:T(8,128)(2,1)}), bf16[512,256]{1,0:T(8,128)(2,1)}) %reduce-scatter.2.cloned.1.call-update) | async-done | bytes 262160 | tf_op jit(solution)/shard_map/reduce_scatter | solution.py:281
  181.9 24.7 %all-reduce.4 = f32[512,256]{1,0:T(8,128)S(1)} all-reduce(bf16[512,256]{1,0:T(8,128)(2,1)} %reduce-scatter.2.cloned.1.call-done), channel_id=1, replica_groups=mesh['dp'=8,'proto'=4] {'proto'}, use_global_device_ids=true, to_apply=%region_16.17 | all-reduce | flops 131072 | bytes 786432 | tf_op jit(solution)/shard_map/psum | solution.py:294
  207.1 1.6 fusion.9
  (39 shorter events, 4.5 us)
Async XLA Ops:
  7.2 1.8 copy-start.4
  7.2 54.3 %all-gather.7.cloned.1.call-start = ((), (), s32[]{:S(2)}) async-start(), calls=%async_computation.2 | async-start | bytes 4866048 | tf_op jit(solution)/shard_map/all_gather | solution.py:254
  10.1 171.7 %reduce-scatter.2.cloned.1.call-start = ((), (), s32[]{:S(2)}) async-start(), calls=%async_computation.1 | async-start | bytes 2359296 | tf_op jit(solution)/shard_map/reduce_scatter | solution.py:281
  111.0 26.6 %copy-start.3 = (s32[32]{0:T(128)S(1)}, s32[32]{0:T(128)}, u32[]{:S(2)}) copy-start(s32[32]{0:T(128)} %sub.82.starts_ref) | copy-start | bytes 388
  111.0 27.6 %copy-start = (f32[2048,256]{1,0:T(8,128)S(1)}, f32[2048,256]{1,0:T(8,128)}, u32[]{:S(2)}) copy-start(f32[2048,256]{1,0:T(8,128)} %get-tuple-element.14) | copy-start | bytes 6291460
  148.0 1.2 copy-start.1
  176.5 30.5 %copy-start.2 = (s32[4,128]{1,0:T(4,128)S(1)}, s32[4,128]{1,0:T(4,128)}, u32[]{:S(2)}) copy-start(s32[4,128]{1,0:T(4,128)} %param.11) | copy-start | bytes 6148
Sparse Core Ops, SparseCore 0:
  10.2 51.1 all-gather.6
  148.1 33.7 reduce-scatter.1
